TPU v7x, 32 devices: a whole 2x2x4 slice. The times are simulated.
32 devices in a mesh: span: 4 (over x, core), wall: 8 (over z, y).
Axes of the slice: x: 2, y: 2, z: 4, core: 2. Of those that a mesh axis runs over, the one named last changes fastest.
Arguments:
- velocity: float32 [3, 256, 128, 128], P(None, 'wall', 'span'), may hold values from -6 to 6
Outputs:
- velocity_next: float32 [3, 256, 128, 128], P(None, 'wall', 'span')
All inputs are finite; a program needn't handle non-finite values.
Results may differ from a plain program's by a relative error of at most 0.0005.
Values sent between devices are 32-bit elements; how exact they have to be, the bound alone decides.
A program may use at most 64 MiB of HBM per device.

v0:
```python
import jax
import jax.numpy as jnp
from jax import lax
from jax.sharding import PartitionSpec as P

visc_base = 4000.0
smag_gain = 2000.0
adv_step = 0.2


def with_halo(cells, sides, width, closed):
    for axis, dim in sides:
        count = lax.axis_size(axis)
        ends = count if closed else count - 1
        head = lax.slice_in_dim(cells, 0, width, axis=dim)
        tail = lax.slice_in_dim(cells, cells.shape[dim] - width, cells.shape[dim], axis=dim)
        cells = jnp.concatenate(
            [
                lax.ppermute(tail, axis, [(i, (i + 1) % count) for i in range(ends)]),
                cells,
                lax.ppermute(head, axis, [((i + 1) % count, i) for i in range(ends)]),
            ],
            axis=dim,
        )
    return cells


def entering(x, axis, combine, identity, reverse):
    peers, place = (lax.axis_size(axis), lax.axis_index(axis))
    everything = jax.tree.map(lambda part: lax.all_gather(part, axis), x)
    start = jax.tree.map(
        lambda part, zero: jnp.broadcast_to(jnp.asarray(zero, part.dtype), part.shape), x, identity
    )

    def lap(k, before):
        at = peers - 1 - k if reverse else k
        reached = at > place if reverse else at < place
        new = combine(before, jax.tree.map(lambda part: part[at], everything))
        return jax.tree.map(lambda a, b: jnp.where(reached, a, b), new, before)

    return lax.fori_loop(0, peers, lap, start)


def prepare(velocity, along_x, along_y, along_z):
    grads = (along_x, along_y, along_z)
    squares = jnp.zeros_like(velocity[0])
    for i in range(3):
        for j in range(3):
            strain = 0.5 * (grads[j][i] + grads[i][j])
            squares = squares + strain * strain
    strain_mag = jnp.sqrt(2.0 * squares)
    coupling = visc_base + smag_gain * strain_mag
    advect = velocity[0] * along_x + velocity[1] * along_y + velocity[2] * along_z
    return (velocity - adv_step * advect, coupling)


def mat_join(earlier, later):
    result = []
    for i in range(3):
        for k in range(3):
            total = (
                later[i * 3] * earlier[k]
                + later[i * 3 + 1] * earlier[3 + k]
                + later[i * 3 + 2] * earlier[6 + k]
            )
            result.append(total)
    scale = jnp.abs(result[0])
    for entry in result[1:]:
        scale = scale + jnp.abs(entry)
    return tuple((entry / scale for entry in result))


def affine_join(earlier, later):
    return (later[0] + later[1] * earlier[0], later[1] * earlier[1])


def thomas(moved, links):

    def forward(carry, item):
        upper_prev, shift_prev = carry
        source, coeff = item
        denom = 1.0 + 2.0 * coeff + coeff * upper_prev
        upper = -coeff / denom
        shift = (source + coeff * shift_prev) / denom
        return ((upper, shift), (upper, shift))

    start_upper = jnp.zeros(links.shape[1:], jnp.float32)
    start_shift = jnp.zeros(moved.shape[1:], jnp.float32)
    _, (uppers, shifts) = lax.scan(forward, (start_upper, start_shift), (moved, links), unroll=8)

    def backward(x_next, item):
        upper, shift = item
        value = shift - upper * x_next
        return (value, value)

    _, values = lax.scan(backward, start_shift, (uppers, shifts), reverse=True, unroll=8)
    return values


def body(velocity):
    along_x = 0.5 * (jnp.roll(velocity, -1, axis=3) - jnp.roll(velocity, 1, axis=3))
    span_ext = with_halo(velocity, (("span", 2),), 1, True)
    along_z = 0.5 * (span_ext[:, :, 2:] - span_ext[:, :, :-2])
    wall_ext = with_halo(velocity, (("wall", 1),), 1, False)
    along_y = 0.5 * (wall_ext[:, 2:] - wall_ext[:, :-2])
    right_side, coupling = prepare(velocity, along_x, along_y, along_z)
    moved = jnp.moveaxis(right_side, 1, 0)
    links = coupling[:, None]
    count_rows = coupling.shape[0]
    row_index = jnp.arange(count_rows, dtype=jnp.int32).reshape(count_rows, 1, 1, 1)
    edge_low = jnp.where(row_index == 0, links, 0.0)
    edge_high = jnp.where(row_index == count_rows - 1, links, 0.0)
    values = thomas(jnp.concatenate([moved, edge_low, edge_high], axis=1), links)
    base = values[:, :3]
    from_below = values[:, 3:4]
    from_above = values[:, 4:5]
    shape3 = base.shape[1:]
    face_zero = jnp.zeros(shape3, jnp.float32)
    face_one = jnp.ones(shape3, jnp.float32)
    low_base = base[0]
    high_base = base[-1]
    low_below = jnp.broadcast_to(from_below[0], shape3)
    low_above = jnp.broadcast_to(from_above[0], shape3)
    high_below = jnp.broadcast_to(from_below[-1], shape3)
    high_above = jnp.broadcast_to(from_above[-1], shape3)
    matrix = (
        high_below,
        high_below * low_base - high_base * low_below,
        high_base,
        face_zero,
        high_below * low_above - high_above * low_below,
        high_above,
        face_zero,
        -low_below,
        face_one,
    )
    mat_ident = (
        face_one,
        face_zero,
        face_zero,
        face_zero,
        face_one,
        face_zero,
        face_zero,
        face_zero,
        face_one,
    )
    prefix = entering(matrix, "wall", mat_join, mat_ident, False)
    state_s = prefix[2]
    state_t = prefix[5]
    state_q = prefix[8]
    pivot = state_q - low_below * state_t
    offset = (low_base * state_q + low_below * state_s) / pivot
    factor = low_above * state_q / pivot
    incoming = entering((offset, factor), "wall", affine_join, (face_zero, face_one), True)
    above = incoming[0]
    first_value = offset + factor * above
    below = (state_s + state_t * first_value) / state_q
    result = base + from_below * below[None] + from_above * above[None]
    return jnp.moveaxis(result, 0, 1)


def solution(mesh):
    in_specs = (P(None, "wall", "span", None),)
    out_specs = P(None, "wall", "span", None)
    return jax.shard_map(body, mesh=mesh, in_specs=in_specs, out_specs=out_specs, check_vma=False)
```

profile of v0, /device:TPU:0, one launch (start us, length us, event | category | flops | bytes accessed | tf_op | source)
XLA Modules:
  0.0 401.3 jit_solution(4418020224294506419)
XLA Ops:
  0.0 1.5 fusion.127
  2.8 6.1 %collective-permute-start.1 = (f32[3,1,32,128]{3,2,1,0:T(8,128)}, f32[3,1,32,128]{3,2,1,0:T(8,128)}, u32[]{:S(2)}, u32[]{:S(2)}) collective-permute-start(f32[3,1,32,128]{3,2,1,0:T(8,128)} %get-tuple-element.986), channel_id=1, source_target_pairs={{0,1},{1,2},{2,3},{3,4},{4,5},{5,6},{6,7},{8,9},{9,10},{10,11},{11... | collective-permute-start | bytes 147464 | tf_op jit(solution)/shard_map/ppermute | solution.py:19
  8.9 1.8 fusion.128
  11.6 2.7 multiply_bitcast_fusion.2
  14.3 1.7 fusion.125
  16.0 2.2 fusion.126
  19.5 4.2 %subtract_bitcast_fusion = (f32[32,3,32,128]{3,2,0,1:T(8,128)S(1)}, f32[3,32,32,128]{3,2,1,0:T(8,128)S(1)}) fusion(f32[3,32,32,128]{3,2,1,0:T(8,128)S(1)} %copy-done, f32[3,1,32,128]{3,2,1,0:T(8,128)} %collective-permute-done.1, f32[3,1,32,128]{3,2,1,0:T(8,128)} %collective-permute-done, f32[3,32,1,128]{3,2,1,0:T(1,128)} %collective-permute-done.3, ...), kind=kLoop, calls=%fused_computation.201 | loop fusion | flops 6291456 | bytes 9633792 | tf_op jit(solution)/shard_map/transpose | solution.py:107
  23.8 1.6 fusion.80
  26.7 1.8 pad_maximum_fusion
  28.9 76.4 %while.86 = (s32[]{:T(128)}, f32[1,32,128]{2,1,0:T(8,128)}, f32[5,32,128]{2,1,0:T(8,128)S(1)}, f32[4,8,1,32,128]{4,3,1,2,0:T(8,128)}, f32[4,8,5,32,128]{4,3,2,1,...) while((s32[]{:T(128)}, f32[1,32,128]{2,1,0:T(8,128)}, ...), condition=%wide.region_1.2_spmd.clone.clone, body=%wide.region_0.1_spmd.clone.sunk.clone | while | flops 1114120 | bytes 6360982 | solution.py:89
  29.5 1.3 constant_dynamic-update-slice_fusion.25
  30.9 1.3 constant_dynamic-update-slice_fusion.26
  32.2 1.3 constant_dynamic-update-slice_fusion.27
  33.6 1.3 constant_dynamic-update-slice_fusion.28
  34.9 1.3 constant_dynamic-update-slice_fusion.29
  36.2 1.3 constant_dynamic-update-slice_fusion.30
  47.5 1.3 constant_dynamic-update-slice_fusion.24
  66.8 1.3 constant_dynamic-update-slice_fusion.24
  68.1 1.3 constant_dynamic-update-slice_fusion.25
  69.4 1.3 constant_dynamic-update-slice_fusion.26
  70.8 1.3 constant_dynamic-update-slice_fusion.27
  72.1 1.3 constant_dynamic-update-slice_fusion.28
  73.5 1.3 constant_dynamic-update-slice_fusion.29
  86.0 1.3 constant_dynamic-update-slice_fusion.24
  90.1 1.3 constant_dynamic-update-slice_fusion.27
  91.4 1.3 constant_dynamic-update-slice_fusion.28
  105.3 1.8 broadcast.388
  107.1 8.1 %while.87 = (s32[]{:T(128)}, f32[5,32,128]{2,1,0:T(8,128)S(1)}, f32[4,8,5,32,128]{4,3,2,1,0:T(8,128)}, f32[4,8,5,32,128]{4,3,2,1,0:T(8,128)S(1)}, f32[4,8,1,32,128]{4,3,2,1,0:T(8,128)}) while((s32[]{:T(128)}, f32[5,32,128]{2,1,0:T(8,128)S(1)}, f32[4,8,5,32,128]{4,3,2,1,0:T(8,128)}, f32[4,8,5,32,128]{4,3,2,1,0:T(8,128)S(1)}, ...), condition=%wide.region_3.4_spmd.clone.clone, body=%wide.region_2.3_spmd.clone.sunk.clone | while | flops 532490 | bytes 4555020 | solution.py:96
  116.8 2.2 slice_bitcast_fusion.1
  119.8 33.6 %all_gather.41 = f32[8,3,32,128]{3,2,1,0:T(8,128)} all-gather(f32[1,3,32,128]{3,2,1,0:T(8,128)S(1)} %get-tuple-element.969), channel_id=1, replica_groups=mesh['span'=4,'wall'=8] {'wall'}, dimensions={0}, use_global_device_ids=true | all-gather | bytes 442368 | tf_op jit(solution)/shard_map/all_gather | solution.py:30
  153.5 33.3 %all_gather.42 = f32[8,3,32,128]{3,2,1,0:T(8,128)} all-gather(f32[1,3,32,128]{3,2,1,0:T(8,128)S(1)} %get-tuple-element.968), channel_id=1, replica_groups=mesh['span'=4,'wall'=8] {'wall'}, dimensions={0}, use_global_device_ids=true | all-gather | bytes 442368 | tf_op jit(solution)/shard_map/all_gather | solution.py:30
  186.7 30.6 %all-gather = f32[8,1,32,128]{3,2,1,0:T(8,128)S(1)} all-gather(f32[1,1,32,128]{3,2,1,0:T(8,128)S(1)} %get-tuple-element.965), channel_id=6, replica_groups=mesh['span'=4,'wall'=8] {'wall'}, dimensions={0}, use_global_device_ids=true | all-gather | bytes 147456 | tf_op jit(solution)/shard_map/all_gather | solution.py:30
  217.3 30.6 %all-gather.2 = f32[8,1,32,128]{3,2,1,0:T(8,128)S(1)} all-gather(f32[1,1,32,128]{3,2,1,0:T(8,128)S(1)} %get-tuple-element.963), channel_id=8, replica_groups=mesh['span'=4,'wall'=8] {'wall'}, dimensions={0}, use_global_device_ids=true | all-gather | bytes 147456 | tf_op jit(solution)/shard_map/all_gather | solution.py:30
  248.0 30.5 %all-gather.1 = f32[256,128]{1,0:T(8,128)S(1)} all-gather(f32[32,128]{1,0:T(8,128)S(1)} %get-tuple-element.967), channel_id=7, replica_groups=mesh['span'=4,'wall'=8] {'wall'}, dimensions={0}, use_global_device_ids=true | all-gather | bytes 147456 | tf_op jit(solution)/shard_map/all_gather | solution.py:30
  278.5 30.5 %all-gather.3 = f32[256,128]{1,0:T(8,128)S(1)} all-gather(f32[32,128]{1,0:T(8,128)S(1)} %get-tuple-element.966), channel_id=9, replica_groups=mesh['span'=4,'wall'=8] {'wall'}, dimensions={0}, use_global_device_ids=true | all-gather | bytes 147456 | tf_op jit(solution)/shard_map/all_gather | solution.py:30
  312.2 14.6 %while.88 = (s32[]{:T(128)}, f32[3,32,128]{2,1,0:T(8,128)S(1)}, f32[3,32,128]{2,1,0:T(8,128)S(1)}, f32[3,32,128]{2,1,0:T(8,128)S(1)}, f32[3,32,128]{2,1,0:T(8,12...) while((s32[]{:T(128)}, f32[3,32,128]{2,1,0:T(8,128)S(1)}, ...), condition=%wide.region_5.6_spmd.clone.clone, body=%wide.region_4.5_spmd.clone.sunk.clone | while | flops 1118212 | bytes 2457783 | solution.py:41
  312.2 1.8 divide_select_fusion.13
  314.1 1.7 divide_select_fusion.13
  315.9 1.7 divide_select_fusion.13
  317.8 1.7 divide_select_fusion.13
  319.6 1.7 divide_select_fusion.13
  321.4 1.7 divide_select_fusion.13
  323.2 1.7 divide_select_fusion.13
  325.0 1.7 divide_select_fusion.13
  327.7 31.0 %all-gather.4 = f32[24,32,128]{2,1,0:T(8,128)S(1)} all-gather(f32[3,32,128]{2,1,0:T(8,128)S(1)} %get-tuple-element.990), channel_id=10, replica_groups=mesh['span'=4,'wall'=8] {'wall'}, dimensions={0}, use_global_device_ids=true | all-gather | bytes 442368 | tf_op jit(solution)/shard_map/all_gather | solution.py:30
  358.7 33.0 %all-gather.5 = f32[24,32,128]{2,1,0:T(8,128)} all-gather(f32[3,32,128]{2,1,0:T(8,128)S(1)} %get-tuple-element.989), channel_id=11, replica_groups=mesh['span'=4,'wall'=8] {'wall'}, dimensions={0}, use_global_device_ids=true | all-gather | bytes 442368 | tf_op jit(solution)/shard_map/all_gather | solution.py:30
  391.6 6.8 %while.89 = (s32[]{:T(128)}, f32[3,32,128]{2,1,0:T(8,128)S(1)}, s32[]{:T(128)}, f32[8,3,32,128]{3,2,1,0:T(8,128)S(1)}, f32[8,3,32,128]{3,2,1,0:T(8,128)}) while((s32[]{:T(128)}, f32[3,32,128]{2,1,0:T(8,128)S(1)}, s32[]{:T(128)}, f32[8,3,32,128]{3,2,1,0:T(8,128)S(1)}, f32[8,3,32,128]{3,2,1,0:T(8,128)}) %tuple.287), condition=%wide.region_7.8_spmd.clone.clone, body=%wide.region_6.7_spmd.clone.sunk.clone | while | flops 49160 | bytes 196739 | solution.py:41
  398.5 1.5 fusion.77
  (196 shorter events, 82.5 us)
Async XLA Ops:
  1.5 18.0 %collective-permute-start = (f32[3,1,32,128]{3,2,1,0:T(8,128)}, f32[3,1,32,128]{3,2,1,0:T(8,128)}, u32[]{:S(2)}, u32[]{:S(2)}) collective-permute-start(f32[3,1,32,128]{3,2,1,0:T(8,128)} %get-tuple-element.985), channel_id=1, source_target_pairs={{1,0},{2,1},{3,2},{4,3},{5,4},{6,5},{7,6},{9,8},{10,9},{11,10},{12... | collective-permute-start | bytes 147464 | tf_op jit(solution)/shard_map/ppermute | solution.py:21
  2.8 16.7 %collective-permute-start.1 = (f32[3,1,32,128]{3,2,1,0:T(8,128)}, f32[3,1,32,128]{3,2,1,0:T(8,128)}, u32[]{:S(2)}, u32[]{:S(2)}) collective-permute-start(f32[3,1,32,128]{3,2,1,0:T(8,128)} %get-tuple-element.986), channel_id=1, source_target_pairs={{0,1},{1,2},{2,3},{3,4},{4,5},{5,6},{6,7},{8,9},{9,10},{10,11},{11... | collective-permute-start | bytes 147464 | tf_op jit(solution)/shard_map/ppermute | solution.py:19
  10.7 8.7 %collective-permute-start.2 = (f32[3,32,1,128]{3,2,1,0:T(1,128)}, f32[3,32,1,128]{3,2,1,0:T(1,128)}, u32[]{:S(2)}, u32[]{:S(2)}) collective-permute-start(f32[3,32,1,128]{3,2,1,0:T(1,128)} %get-tuple-element.987), channel_id=1, source_target_pairs={{8,0},{16,8},{24,16},{0,24},{9,1},{17,9},{25,17},{1,25},{10,2},{18... | collective-permute-start | bytes 147464 | tf_op jit(solution)/shard_map/ppermute | solution.py:21
  11.6 2.7 copy-start
  11.6 7.9 %collective-permute-start.3 = (f32[3,32,1,128]{3,2,1,0:T(1,128)}, f32[3,32,1,128]{3,2,1,0:T(1,128)}, u32[]{:S(2)}, u32[]{:S(2)}) collective-permute-start(f32[3,32,1,128]{3,2,1,0:T(1,128)} %get-tuple-element.988), channel_id=1, source_target_pairs={{0,8},{8,16},{16,24},{24,0},{1,9},{9,17},{17,25},{25,1},{2,10},{10... | collective-permute-start | bytes 147464 | tf_op jit(solution)/shard_map/ppermute | solution.py:19
  25.3 0.7 copy-start.10
  26.0 0.6 copy-start.9
  41.3 4.9 %copy-start.5 = (f32[8,1,32,128]{3,2,0,1:T(8,128)S(1)}, f32[8,1,32,128]{3,2,0,1:T(8,128)}, u32[]{:S(2)}) copy-start(f32[8,1,32,128]{3,2,0,1:T(8,128)} %get-tuple-element.1362) | copy-start | bytes 393220 | tf_op jit(solution)/shard_map/while
  41.3 4.9 %copy-start.6 = (f32[1,32,128]{2,1,0:T(8,128)S(1)}, f32[1,32,128]{2,1,0:T(8,128)}, u32[]{:S(2)}) copy-start(f32[1,32,128]{2,1,0:T(8,128)} %get-tuple-element.1363) | copy-start | bytes 49156 | tf_op jit(solution)/shard_map/while
  60.6 4.9 %copy-start.5 = (f32[8,1,32,128]{3,2,0,1:T(8,128)S(1)}, f32[8,1,32,128]{3,2,0,1:T(8,128)}, u32[]{:S(2)}) copy-start(f32[8,1,32,128]{3,2,0,1:T(8,128)} %get-tuple-element.1362) | copy-start | bytes 393220 | tf_op jit(solution)/shard_map/while
  60.6 4.9 %copy-start.6 = (f32[1,32,128]{2,1,0:T(8,128)S(1)}, f32[1,32,128]{2,1,0:T(8,128)}, u32[]{:S(2)}) copy-start(f32[1,32,128]{2,1,0:T(8,128)} %get-tuple-element.1363) | copy-start | bytes 49156 | tf_op jit(solution)/shard_map/while
  79.9 4.9 %copy-start.5 = (f32[8,1,32,128]{3,2,0,1:T(8,128)S(1)}, f32[8,1,32,128]{3,2,0,1:T(8,128)}, u32[]{:S(2)}) copy-start(f32[8,1,32,128]{3,2,0,1:T(8,128)} %get-tuple-element.1362) | copy-start | bytes 393220 | tf_op jit(solution)/shard_map/while
  79.9 4.9 %copy-start.6 = (f32[1,32,128]{2,1,0:T(8,128)S(1)}, f32[1,32,128]{2,1,0:T(8,128)}, u32[]{:S(2)}) copy-start(f32[1,32,128]{2,1,0:T(8,128)} %get-tuple-element.1363) | copy-start | bytes 49156 | tf_op jit(solution)/shard_map/while
  99.1 4.9 %copy-start.5 = (f32[8,1,32,128]{3,2,0,1:T(8,128)S(1)}, f32[8,1,32,128]{3,2,0,1:T(8,128)}, u32[]{:S(2)}) copy-start(f32[8,1,32,128]{3,2,0,1:T(8,128)} %get-tuple-element.1362) | copy-start | bytes 393220 | tf_op jit(solution)/shard_map/while
  99.2 4.9 %copy-start.6 = (f32[1,32,128]{2,1,0:T(8,128)S(1)}, f32[1,32,128]{2,1,0:T(8,128)}, u32[]{:S(2)}) copy-start(f32[1,32,128]{2,1,0:T(8,128)} %get-tuple-element.1363) | copy-start | bytes 49156 | tf_op jit(solution)/shard_map/while
  153.5 158.7 %copy-start.2 = (f32[3,32,128]{2,1,0:T(8,128)S(1)}, f32[3,32,128]{2,1,0:T(8,128)}, u32[]{:S(2)}) copy-start(f32[3,32,128]{2,1,0:T(8,128)} %custom-call.6) | copy-start | bytes 147460
  153.5 158.7 %copy-start.3 = (f32[3,32,128]{2,1,0:T(8,128)S(1)}, f32[3,32,128]{2,1,0:T(8,128)}, u32[]{:S(2)}) copy-start(f32[3,32,128]{2,1,0:T(8,128)} %custom-call.7) | copy-start | bytes 147460
  153.5 158.7 %copy-start.4 = (f32[3,32,128]{2,1,0:T(8,128)S(1)}, f32[3,32,128]{2,1,0:T(8,128)}, u32[]{:S(2)}) copy-start(f32[3,32,128]{2,1,0:T(8,128)} %custom-call.9) | copy-start | bytes 147460
  311.4 15.4 %copy-start.1 = (f32[4,8,5,32,128]{4,3,2,1,0:T(8,128)S(1)}, f32[4,8,5,32,128]{4,3,2,1,0:T(8,128)}, u32[]{:S(2)}) copy-start(f32[4,8,5,32,128]{4,3,2,1,0:T(8,128)} %get-tuple-element.665) | copy-start | bytes 7864324
  312.2 79.4 %copy-start.7 = (f32[3,32,128]{2,1,0:T(8,128)S(1)}, f32[3,32,128]{2,1,0:T(8,128)}, u32[]{:S(2)}) copy-start(f32[3,32,128]{2,1,0:T(8,128)} %custom-call.12) | copy-start | bytes 147460
  326.8 71.6 %copy-start.8 = (f32[3,32,128]{2,1,0:T(8,128)S(1)}, f32[3,32,128]{2,1,0:T(8,128)}, u32[]{:S(2)}) copy-start(f32[3,32,128]{2,1,0:T(8,128)} %get-tuple-element.668) | copy-start | bytes 147460
where the time goes:
time: 406 us; the launch traced here: 401 us
  blocking collectives  253 us (62%)
  other arithmetic  111 us (27%)
  local copies, waits for them, and re-layouts  27.5 us (7%)
  starting transfers between devices  8.28 us (2%)
    all_gather x8, blocking collectives, entering(): everything = jax.tree.map(lambda part: lax.all_gather(part, axis), x)  253 us
    while x72, other arithmetic  63.8 us
    select_n x24, other arithmetic, lap(): return jax.tree.map(lambda a, b: jnp.where(reached, a, b), new, before)  21 us
  transfers between devices with their start and end apart: 4, of which 0 were waited for; matrix products, arithmetic and copies ran while one was open for 2% of the time, Pallas kernels for 0%

commit v1 on v0

v1 whole, which is shorter than its diff:
```python
import functools

import jax
import jax.numpy as jnp
from jax import lax
from jax.experimental import pallas as pl
from jax.experimental.pallas import tpu as pltpu
from jax.sharding import PartitionSpec as P

visc_base = 4000.0
smag_gain = 2000.0
adv_step = 0.2

MESH = pl.DeviceIdType.MESH


def inverse(x):
    guess = pl.reciprocal(x, approx=True)
    return guess * (2.0 - x * guess)


def kernel(
    n, m, vel, out, ext, zsend, zlo, zhi, fac_u, fac_p, fac_s, part, parts, ends, sides, planes,
    load_sem, zs_sem, zr_sem, ys_sem, yr_sem, ps_sem, pr_sem, es_sem, er_sem, out_sem,
):
    _, ny, nz, nx = vel.shape
    rows = nz // n
    me = lax.axis_index("wall")
    mine = lax.axis_index("span")
    after, before = lax.rem(mine + 1, m), lax.rem(mine + m - 1, m)

    load = pltpu.make_async_copy(vel, ext.at[:, pl.ds(1, ny)], load_sem)
    load.start()

    barrier = pltpu.get_barrier_semaphore()
    for hop in range(1, n):
        pl.semaphore_signal(
            barrier, inc=1, device_id={"wall": lax.rem(me + hop, n)}, device_id_type=MESH
        )
    for peer in (after, before):
        pl.semaphore_signal(barrier, inc=1, device_id={"span": peer}, device_id_type=MESH)
    pl.semaphore_wait(barrier, n + 1)

    up = pltpu.make_async_remote_copy(
        vel.at[:, ny - 1], ext.at[:, 0], ys_sem.at[0], yr_sem.at[0],
        device_id={"wall": jnp.minimum(me + 1, n - 1)}, device_id_type=MESH,
    )
    down = pltpu.make_async_remote_copy(
        vel.at[:, 0], ext.at[:, ny + 1], ys_sem.at[1], yr_sem.at[1],
        device_id={"wall": jnp.maximum(me - 1, 0)}, device_id_type=MESH,
    )
    has_above = me < n - 1
    has_below = me > 0
    load.wait()

    for c in range(3):
        zsend[0, c] = ext[c, pl.ds(1, ny), 0, :]
        zsend[1, c] = ext[c, pl.ds(1, ny), nz - 1, :]
    to_after = pltpu.make_async_remote_copy(
        zsend.at[1], zlo, zs_sem.at[1], zr_sem.at[1],
        device_id={"span": after}, device_id_type=MESH,
    )
    to_before = pltpu.make_async_remote_copy(
        zsend.at[0], zhi, zs_sem.at[0], zr_sem.at[0],
        device_id={"span": before}, device_id_type=MESH,
    )
    to_after.start()
    to_before.start()
    pl.when(has_above)(up.start)
    pl.when(has_below)(down.start)

    depth = lax.broadcasted_iota(jnp.int32, (nz, nx), 0)
    is_first = depth == 0
    is_last = depth == nz - 1

    def prepare(y):
        v, hx, hy, hz = [], [], [], []
        for c in range(3):
            here = ext[c, y + 1]
            v.append(here)
            hx.append(pltpu.roll(here, nx - 1, 1) - pltpu.roll(here, 1, 1))
            hy.append(ext[c, y + 2] - ext[c, y])
            ahead = jnp.where(is_last, zhi[c, pl.ds(y, 1)], pltpu.roll(here, nz - 1, 0))
            behind = jnp.where(is_first, zlo[c, pl.ds(y, 1)], pltpu.roll(here, 1, 0))
            hz.append(ahead - behind)
        xy = hx[1] + hy[0]
        xz = hx[2] + hz[0]
        yz = hy[2] + hz[1]
        squares = 2.0 * (hx[0] * hx[0] + hy[1] * hy[1] + hz[2] * hz[2])
        squares = squares + (xy * xy + xz * xz + yz * yz)
        strain = squares * lax.rsqrt(jnp.maximum(squares, 1e-30))
        e = inverse(visc_base + (0.5 * smag_gain) * strain)
        f = []
        for c in range(3):
            advect = v[0] * hx[c] + v[1] * hy[c] + v[2] * hz[c]
            f.append((v[c] - (0.5 * adv_step) * advect) * e)
        return e, f

    def step(y, carry):
        w, p, left, s, a = carry
        e, f = prepare(y)
        t = e + w
        u = inverse(1.0 + t)
        w = t * u
        s = tuple((s[c] + f[c]) * u for c in range(3))
        a = tuple(a[c] + p * s[c] for c in range(3))
        p_new = p * u
        left = left - p * p_new
        fac_u[y] = u
        fac_p[y] = p_new
        for c in range(3):
            fac_s[c, y] = s[c]
        return w, p_new, left, s, a

    to_after.wait_recv()
    to_before.wait_recv()
    one = jnp.ones((nz, nx), jnp.float32)
    zero = jnp.zeros((nz, nx), jnp.float32)
    carry = (one, one, one, (zero,) * 3, (zero,) * 3)
    carry = lax.fori_loop(1, ny - 1, step, carry)

    @pl.when(has_above)
    def _():
        down.wait_recv()

    @pl.when(has_below)
    def _():
        up.wait_recv()

    @pl.when(jnp.logical_not(has_above))
    def _():
        ext[:, ny + 1] = jnp.zeros((3, nz, nx), jnp.float32)

    @pl.when(jnp.logical_not(has_below))
    def _():
        ext[:, 0] = jnp.zeros((3, nz, nx), jnp.float32)

    w, p, left, s, a = step(ny - 1, carry)
    e, f = prepare(0)
    values = (e + left, w, p, *s, *(f[c] + a[c] for c in range(3)))
    for k in range(n):
        for j, value in enumerate(values):
            part[k, j * rows : (j + 1) * rows] = value[k * rows : (k + 1) * rows]

    def spread(src, dst, send, recv):
        copies = []
        for hop in range(1, n):
            to = lax.rem(me + hop, n)
            copies.append(
                pltpu.make_async_remote_copy(
                    src.at[to], dst.at[me], send.at[to], recv.at[me],
                    device_id={"wall": to}, device_id_type=MESH,
                )
            )
        return copies

    def arrived(src, dst, send, recv, k):
        @pl.when(me != k)
        def _():
            pltpu.make_async_remote_copy(
                src.at[k], dst.at[k], send.at[k], recv.at[k],
                device_id={"wall": k}, device_id_type=MESH,
            ).wait_recv()

    first = spread(part, parts, ps_sem, pr_sem)
    for copy in first:
        copy.start()
    parts[me] = part[me]

    def item(k, j):
        return parts[k, j * rows : (j + 1) * rows]

    ratios, shifts = [], []
    for k in range(n):
        arrived(part, parts, ps_sem, pr_sem, k)
        if k == 0:
            scale = inverse(item(0, 0) + 1.0)
            shift = [item(0, 6 + c) * scale for c in range(3)]
        else:
            p_low = item(k - 1, 2)
            scale = inverse(item(k, 0) + (item(k - 1, 1) - p_low * ratios[-1]))
            shift = [
                (item(k, 6 + c) + item(k - 1, 3 + c) + p_low * shifts[-1][c]) * scale
                for c in range(3)
            ]
        ratios.append(item(k, 2) * scale)
        shifts.append(shift)
    above = [jnp.zeros((rows, nx), jnp.float32)] * 3
    for k in reversed(range(n)):
        here = [shifts[k][c] + ratios[k] * above[c] for c in range(3)]
        for c in range(3):
            ends[k, c * rows : (c + 1) * rows] = here[c]
            ends[k, (3 + c) * rows : (4 + c) * rows] = above[c]
        above = here
    second = spread(ends, sides, es_sem, er_sem)
    for copy in second:
        copy.start()
    sides[me] = ends[me]
    for k in range(n):
        arrived(ends, sides, es_sem, er_sem, k)
        for j in range(6):
            planes[j, k * rows : (k + 1) * rows] = sides[k, j * rows : (j + 1) * rows]

    base = tuple(planes[c] for c in range(3))

    def back(i, x):
        y = ny - 1 - i
        u = fac_u[y]
        p = fac_p[y]
        x = tuple(fac_s[c, y] + p * base[c] + u * x[c] for c in range(3))
        for c in range(3):
            fac_s[c, y] = x[c]
        return x

    lax.fori_loop(0, ny - 1, back, tuple(planes[3 + c] for c in range(3)))
    for c in range(3):
        fac_s[c, 0] = base[c]
    store = pltpu.make_async_copy(fac_s, out, out_sem)
    store.start()

    to_after.wait_send()
    to_before.wait_send()
    pl.when(has_above)(up.wait_send)
    pl.when(has_below)(down.wait_send)
    for copy in first + second:
        copy.wait_send()
    store.wait()


def body(n, m, velocity):
    _, ny, nz, nx = velocity.shape
    rows = nz // n
    f32 = jnp.float32
    dma = pltpu.SemaphoreType.DMA
    return pl.pallas_call(
        functools.partial(kernel, n, m),
        out_shape=jax.ShapeDtypeStruct(velocity.shape, f32),
        in_specs=[pl.BlockSpec(memory_space=pl.ANY)],
        out_specs=pl.BlockSpec(memory_space=pl.ANY),
        scratch_shapes=[
            pltpu.VMEM((3, ny + 2, nz, nx), f32),
            pltpu.VMEM((2, 3, ny, nx), f32),
            pltpu.VMEM((3, ny, nx), f32),
            pltpu.VMEM((3, ny, nx), f32),
            pltpu.VMEM((ny, nz, nx), f32),
            pltpu.VMEM((ny, nz, nx), f32),
            pltpu.VMEM((3, ny, nz, nx), f32),
            pltpu.VMEM((n, 9 * rows, nx), f32),
            pltpu.VMEM((n, 9 * rows, nx), f32),
            pltpu.VMEM((n, 6 * rows, nx), f32),
            pltpu.VMEM((n, 6 * rows, nx), f32),
            pltpu.VMEM((6, nz, nx), f32),
            dma,
            dma((2,)),
            dma((2,)),
            dma((2,)),
            dma((2,)),
            dma((n,)),
            dma((n,)),
            dma((n,)),
            dma((n,)),
            dma,
        ],
        compiler_params=pltpu.CompilerParams(
            collective_id=0, has_side_effects=True, vmem_limit_bytes=32 * 1024 * 1024
        ),
        name="channel",
    )(velocity)


def solution(mesh):
    n, m = mesh.shape["wall"], mesh.shape["span"]
    spec = P(None, "wall", "span", None)
    return jax.shard_map(
        functools.partial(body, n, m), mesh=mesh, in_specs=(spec,), out_specs=spec, check_vma=False
    )
```

time: 406 us -> 27 us (0.07); the launches traced: 401 us -> 26.9 us
  blocking collectives: 253 us -> 0 us
  other arithmetic: 111 us -> 0 us
  local copies, waits for them, and re-layouts: 27.5 us -> 2.55 us
  Pallas kernels: 0 us -> 24.3 us
  starting transfers between devices: 8.28 us -> 0 us
    all_gather x8 -> x0, blocking collectives: 253 us -> none  [entering(): everything = jax.tree.map(lambda part: lax.all_gather(part, axis), x)]
    while x72 -> x0, other arithmetic: 63.8 us -> none
    pallas_call x0 -> x1, Pallas kernels: none -> 24.3 us  [body(): pl.pallas_call(functools.partial(kernel, n, m), out_shape=jax.ShapeDtypeS...]
    select_n x26 -> x0, other arithmetic: 21.5 us -> none  [the longest x24 21 us: lap(): return jax.tree.map(lambda a, b: jnp.where(reached, a, b), new, before)]
    ppermute x4 -> x0, starting transfers between devices: 8.28 us -> none  [the longest x2 6.13 us: with_halo(): lax.ppermute(tail, axis, [(i, (i + 1) % count) for i in range(ends)])]
    concatenate x13 -> x0, other arithmetic: 8.26 us -> none  [the longest x8 6.36 us: thomas(): lax.scan(forward, (start_upper, start_shift), (moved, links), unroll=8)]
    slice x4 -> x0, local copies, waits for them, and re-layouts: 7.25 us -> none  [the longest x2 3.96 us: body(): jnp.roll(velocity, -1, axis=3) - jnp.roll(velocity, 1, axis=3)]
    dynamic_update_slice x12 -> x0, local copies, waits for them, and re-layouts: 6.46 us -> none  [thomas(): lax.scan(forward, (start_upper, start_shift), (moved, links), unroll=8)]
  transfers between devices with their start and end apart: 4 -> 0, of which waited for: 0 -> 0; matrix products, arithmetic and copies ran while one was open for 2% -> 0% of each run, Pallas kernels for 0% -> 0%
where the time goes in v1:
time: 27 us; the launch traced here: 26.9 us
  Pallas kernels  24.3 us (90%)
  local copies, waits for them, and re-layouts  2.55 us (9%)
    pallas_call x1, Pallas kernels, body(): pl.pallas_call(functools.partial(kernel, n, m), out_shape=jax.ShapeDtypeS...  24.3 us
    unnamed x3, local copies, waits for them, and re-layouts  2.55 us

profile of v1, /device:TPU:0, one launch (start us, length us, event | category | flops | bytes accessed | tf_op | source)
XLA Modules:
  0.0 26.9 jit_solution(10022809854148986444)
XLA Ops:
  0.0 0.0 copy-start
  0.0 1.4 %copy-done = f32[3,32,32,128]{3,2,1,0:T(8,128)S(1)} copy-done((f32[3,32,32,128]{3,2,1,0:T(8,128)S(1)}, f32[3,32,32,128]{3,2,1,0:T(8,128)}, u32[]{:S(2)}) %copy-start) | copy-done | bytes 1572888
  1.4 24.3 %channel.1 = f32[3,32,32,128]{3,2,1,0:T(8,128)S(1)} custom-call(f32[3,32,32,128]{3,2,1,0:T(8,128)S(1)} %copy-done), custom_call_target="tpu_custom_call" | custom-call | tf_op jit(solution)/shard_map/channel/pallas_call | solution.py:235
  25.8 1.1 %copy.3 = f32[3,32,32,128]{3,2,1,0:T(8,128)} copy(f32[3,32,32,128]{3,2,1,0:T(8,128)S(1)} %channel.1) | data formatting | bytes 3145728
Async XLA Ops:
  0.0 1.4 %copy-start = (f32[3,32,32,128]{3,2,1,0:T(8,128)S(1)}, f32[3,32,32,128]{3,2,1,0:T(8,128)}, u32[]{:S(2)}) copy-start(f32[3,32,32,128]{3,2,1,0:T(8,128)} %vel.1) | copy-start | bytes 4718596

commit v2 on v1

--- a/solution.py
+++ b/solution.py
@@ -12,6 +12,7 @@
 adv_step = 0.2
 
 MESH = pl.DeviceIdType.MESH
+TILE = 8
 
 
 def inverse(x):
@@ -21,41 +22,37 @@
 
 def kernel(
     n, m, vel, out, ext, zsend, zlo, zhi, fac_u, fac_p, fac_s, part, parts, ends, sides, planes,
-    load_sem, zs_sem, zr_sem, ys_sem, yr_sem, ps_sem, pr_sem, es_sem, er_sem, out_sem,
+    load_sem, zs_sem, zr_sem, ys_sem, yr_sem, ps_sem, pr_sem, es_sem, er_sem,
 ):
     _, ny, nz, nx = vel.shape
     rows = nz // n
     me = lax.axis_index("wall")
     mine = lax.axis_index("span")
+    def peer(hop):
+        if n & (n - 1):
+            return lax.rem(me + hop, n)
+        other = me
+        for bit in (1 << i for i in range(n.bit_length() - 1)):
+            if (n - hop) & bit:
+                other = other + bit - 2 * bit * ((me // bit) % 2)
+        return other
+
     after, before = lax.rem(mine + 1, m), lax.rem(mine + m - 1, m)
 
-    load = pltpu.make_async_copy(vel, ext.at[:, pl.ds(1, ny)], load_sem)
+    load = pltpu.make_async_copy(vel, ext.at[:, pl.ds(1, ny), pl.ds(TILE, nz)], load_sem)
     load.start()
 
     barrier = pltpu.get_barrier_semaphore()
     for hop in range(1, n):
-        pl.semaphore_signal(
-            barrier, inc=1, device_id={"wall": lax.rem(me + hop, n)}, device_id_type=MESH
-        )
-    for peer in (after, before):
-        pl.semaphore_signal(barrier, inc=1, device_id={"span": peer}, device_id_type=MESH)
+        pl.semaphore_signal(barrier, inc=1, device_id={"wall": peer(hop)}, device_id_type=MESH)
+    for side in (after, before):
+        pl.semaphore_signal(barrier, inc=1, device_id={"span": side}, device_id_type=MESH)
+
+    load.wait()
+    for c in range(3):
+        zsend[0, c] = ext[c, pl.ds(1, ny), TILE, :]
+        zsend[1, c] = ext[c, pl.ds(1, ny), TILE + nz - 1, :]
     pl.semaphore_wait(barrier, n + 1)
-
-    up = pltpu.make_async_remote_copy(
-        vel.at[:, ny - 1], ext.at[:, 0], ys_sem.at[0], yr_sem.at[0],
-        device_id={"wall": jnp.minimum(me + 1, n - 1)}, device_id_type=MESH,
-    )
-    down = pltpu.make_async_remote_copy(
-        vel.at[:, 0], ext.at[:, ny + 1], ys_sem.at[1], yr_sem.at[1],
-        device_id={"wall": jnp.maximum(me - 1, 0)}, device_id_type=MESH,
-    )
-    has_above = me < n - 1
-    has_below = me > 0
-    load.wait()
-
-    for c in range(3):
-        zsend[0, c] = ext[c, pl.ds(1, ny), 0, :]
-        zsend[1, c] = ext[c, pl.ds(1, ny), nz - 1, :]
     to_after = pltpu.make_async_remote_copy(
         zsend.at[1], zlo, zs_sem.at[1], zr_sem.at[1],
         device_id={"span": after}, device_id_type=MESH,
@@ -66,23 +63,33 @@
     )
     to_after.start()
     to_before.start()
+
+    up = pltpu.make_async_remote_copy(
+        vel.at[:, ny - 1], ext.at[:, 0, pl.ds(TILE, nz)], ys_sem.at[0], yr_sem.at[0],
+        device_id={"wall": jnp.minimum(me + 1, n - 1)}, device_id_type=MESH,
+    )
+    down = pltpu.make_async_remote_copy(
+        vel.at[:, 0], ext.at[:, ny + 1, pl.ds(TILE, nz)], ys_sem.at[1], yr_sem.at[1],
+        device_id={"wall": jnp.maximum(me - 1, 0)}, device_id_type=MESH,
+    )
+    has_above = me < n - 1
+    has_below = me > 0
     pl.when(has_above)(up.start)
     pl.when(has_below)(down.start)
 
-    depth = lax.broadcasted_iota(jnp.int32, (nz, nx), 0)
-    is_first = depth == 0
-    is_last = depth == nz - 1
-
-    def prepare(y):
+    def prepare(y, z):
         v, hx, hy, hz = [], [], [], []
         for c in range(3):
-            here = ext[c, y + 1]
+            here = ext[c, y + 1, z + TILE : z + 2 * TILE]
             v.append(here)
             hx.append(pltpu.roll(here, nx - 1, 1) - pltpu.roll(here, 1, 1))
-            hy.append(ext[c, y + 2] - ext[c, y])
-            ahead = jnp.where(is_last, zhi[c, pl.ds(y, 1)], pltpu.roll(here, nz - 1, 0))
-            behind = jnp.where(is_first, zlo[c, pl.ds(y, 1)], pltpu.roll(here, 1, 0))
-            hz.append(ahead - behind)
+            hy.append(
+                ext[c, y + 2, z + TILE : z + 2 * TILE] - ext[c, y, z + TILE : z + 2 * TILE]
+            )
+            hz.append(
+                ext[c, y + 1, z + TILE + 1 : z + 2 * TILE + 1]
+                - ext[c, y + 1, z + TILE - 1 : z + 2 * TILE - 1]
+            )
         xy = hx[1] + hy[0]
         xz = hx[2] + hz[0]
         yz = hy[2] + hz[1]
@@ -96,9 +103,9 @@
             f.append((v[c] - (0.5 * adv_step) * advect) * e)
         return e, f
 
-    def step(y, carry):
+    def step(y, z, carry):
         w, p, left, s, a = carry
-        e, f = prepare(y)
+        e, f = prepare(y, z)
         t = e + w
         u = inverse(1.0 + t)
         w = t * u
@@ -106,18 +113,37 @@
         a = tuple(a[c] + p * s[c] for c in range(3))
         p_new = p * u
         left = left - p * p_new
-        fac_u[y] = u
-        fac_p[y] = p_new
-        for c in range(3):
-            fac_s[c, y] = s[c]
+        fac_u[y, z : z + TILE] = u
+        fac_p[y, z : z + TILE] = p_new
+        for c in range(3):
+            fac_s[c, y, z : z + TILE] = s[c]
         return w, p_new, left, s, a
+
+    one = jnp.ones((TILE, nx), jnp.float32)
+    zero = jnp.zeros((TILE, nx), jnp.float32)
+    start = (one, one, one, (zero,) * 3, (zero,) * 3)
+    burst = 3 if (ny - 2) % 3 == 0 else 1
+
+    def sweep(zs):
+        def some(i, carries):
+            for k in range(burst):
+                carries = tuple(
+                    step(1 + i * burst + k, z, carry) for z, carry in zip(zs, carries)
+                )
+            return carries
+
+        return lax.fori_loop(0, (ny - 2) // burst, some, (start,) * len(zs))
+
+    inner = tuple(range(TILE, nz - TILE, TILE))
+    outer = (0, nz - TILE)
+    carries = dict(zip(inner, sweep(inner)))
 
     to_after.wait_recv()
     to_before.wait_recv()
-    one = jnp.ones((nz, nx), jnp.float32)
-    zero = jnp.zeros((nz, nx), jnp.float32)
-    carry = (one, one, one, (zero,) * 3, (zero,) * 3)
-    carry = lax.fori_loop(1, ny - 1, step, carry)
+    for c in range(3):
+        ext[c, pl.ds(1, ny), TILE - 1, :] = zlo[c]
+        ext[c, pl.ds(1, ny), TILE + nz, :] = zhi[c]
+    carries.update(zip(outer, sweep(outer)))
 
     @pl.when(has_above)
     def _():
@@ -129,23 +155,24 @@
 
     @pl.when(jnp.logical_not(has_above))
     def _():
-        ext[:, ny + 1] = jnp.zeros((3, nz, nx), jnp.float32)
+        ext[:, ny + 1, TILE : TILE + nz] = jnp.zeros((3, nz, nx), jnp.float32)
 
     @pl.when(jnp.logical_not(has_below))
     def _():
-        ext[:, 0] = jnp.zeros((3, nz, nx), jnp.float32)
-
-    w, p, left, s, a = step(ny - 1, carry)
-    e, f = prepare(0)
-    values = (e + left, w, p, *s, *(f[c] + a[c] for c in range(3)))
-    for k in range(n):
-        for j, value in enumerate(values):
-            part[k, j * rows : (j + 1) * rows] = value[k * rows : (k + 1) * rows]
+        ext[:, 0, TILE : TILE + nz] = jnp.zeros((3, nz, nx), jnp.float32)
+
+    for z in range(0, nz, TILE):
+        w, p, left, s, a = step(ny - 1, z, carries[z])
+        e, f = prepare(0, z)
+        values = (e + left, w, p, *s, *(f[c] + a[c] for c in range(3)))
+        for k in range(z // rows, (z + TILE) // rows):
+            for j, value in enumerate(values):
+                part[k, j * rows : (j + 1) * rows] = value[k * rows - z : (k + 1) * rows - z]
 
     def spread(src, dst, send, recv):
         copies = []
         for hop in range(1, n):
-            to = lax.rem(me + hop, n)
+            to = peer(hop)
             copies.append(
                 pltpu.make_async_remote_copy(
                     src.at[to], dst.at[me], send.at[to], recv.at[me],
@@ -209,14 +236,12 @@
         p = fac_p[y]
         x = tuple(fac_s[c, y] + p * base[c] + u * x[c] for c in range(3))
         for c in range(3):
-            fac_s[c, y] = x[c]
+            out[c, y] = x[c]
         return x
 
     lax.fori_loop(0, ny - 1, back, tuple(planes[3 + c] for c in range(3)))
     for c in range(3):
-        fac_s[c, 0] = base[c]
-    store = pltpu.make_async_copy(fac_s, out, out_sem)
-    store.start()
+        out[c, 0] = base[c]
 
     to_after.wait_send()
     to_before.wait_send()
@@ -224,7 +249,6 @@
     pl.when(has_below)(down.wait_send)
     for copy in first + second:
         copy.wait_send()
-    store.wait()
 
 
 def body(n, m, velocity):
@@ -235,10 +259,10 @@
     return pl.pallas_call(
         functools.partial(kernel, n, m),
         out_shape=jax.ShapeDtypeStruct(velocity.shape, f32),
-        in_specs=[pl.BlockSpec(memory_space=pl.ANY)],
-        out_specs=pl.BlockSpec(memory_space=pl.ANY),
+        in_specs=[pl.BlockSpec(memory_space=pltpu.HBM)],
+        out_specs=pl.BlockSpec(memory_space=pltpu.VMEM),
         scratch_shapes=[
-            pltpu.VMEM((3, ny + 2, nz, nx), f32),
+            pltpu.VMEM((3, ny + 2, nz + 2 * TILE, nx), f32),
             pltpu.VMEM((2, 3, ny, nx), f32),
             pltpu.VMEM((3, ny, nx), f32),
             pltpu.VMEM((3, ny, nx), f32),
@@ -259,7 +283,6 @@
             dma((n,)),
             dma((n,)),
             dma((n,)),
-            dma,
         ],
         compiler_params=pltpu.CompilerParams(
             collective_id=0, has_side_effects=True, vmem_limit_bytes=32 * 1024 * 1024

time: 27 us -> 23.2 us (0.86)
  Pallas kernels: 24.3 us -> 20.5 us
    pallas_call x1, Pallas kernels: 24.3 us -> 20.5 us  [body(): pl.pallas_call(functools.partial(kernel, n, m), out_shape=jax.ShapeDtypeS...]
where the time goes in v2:
time: 23.2 us; the launch traced here: 23 us
  Pallas kernels  20.5 us (88%)
  local copies, waits for them, and re-layouts  2.55 us (11%)
    pallas_call x1, Pallas kernels, body(): pl.pallas_call(functools.partial(kernel, n, m), out_shape=jax.ShapeDtypeS...  20.5 us
    unnamed x3, local copies, waits for them, and re-layouts  2.55 us

profile of v2, /device:TPU:0, one launch (start us, length us, event | category | flops | bytes accessed | tf_op | source)
XLA Modules:
  0.0 23.0 jit_solution(15963534845754601581)
XLA Ops:
  0.0 0.0 copy-start
  0.0 1.4 %copy-done = f32[3,32,32,128]{3,2,1,0:T(8,128)S(1)} copy-done((f32[3,32,32,128]{3,2,1,0:T(8,128)S(1)}, f32[3,32,32,128]{3,2,1,0:T(8,128)}, u32[]{:S(2)}) %copy-start) | copy-done | bytes 1572888
  1.4 20.5 %channel.1 = f32[3,32,32,128]{3,2,1,0:T(8,128)S(1)} custom-call(f32[3,32,32,128]{3,2,1,0:T(8,128)S(1)} %copy-done), custom_call_target="tpu_custom_call" | custom-call | tf_op jit(solution)/shard_map/channel/pallas_call | solution.py:259
  21.9 1.1 %copy.3 = f32[3,32,32,128]{3,2,1,0:T(8,128)} copy(f32[3,32,32,128]{3,2,1,0:T(8,128)S(1)} %channel.1) | data formatting | bytes 3145728
Async XLA Ops:
  0.0 1.4 %copy-start = (f32[3,32,32,128]{3,2,1,0:T(8,128)S(1)}, f32[3,32,32,128]{3,2,1,0:T(8,128)}, u32[]{:S(2)}) copy-start(f32[3,32,32,128]{3,2,1,0:T(8,128)} %vel.1) | copy-start | bytes 4718596

commit v3 on v2

--- a/solution.py
+++ b/solution.py
@@ -285,7 +285,7 @@
             dma((n,)),
         ],
         compiler_params=pltpu.CompilerParams(
-            collective_id=0, has_side_effects=True, vmem_limit_bytes=32 * 1024 * 1024
+            collective_id=0, has_side_effects=True, vmem_limit_bytes=52 * 1024 * 1024
         ),
         name="channel",
     )(velocity)

time: 23.2 us -> 21.6 us (0.931)
  local copies, waits for them, and re-layouts: 2.55 us -> 1.15 us
    unnamed x3 -> x1, local copies, waits for them, and re-layouts: 2.55 us -> 1.15 us
where the time goes in v3:
time: 21.6 us; the launch traced here: 21.5 us
  Pallas kernels  20.3 us (94%)
  local copies, waits for them, and re-layouts  1.15 us (5%)
    pallas_call x1, Pallas kernels, body(): pl.pallas_call(functools.partial(kernel, n, m), out_shape=jax.ShapeDtypeS...  20.3 us
    unnamed x1, local copies, waits for them, and re-layouts  1.15 us

profile of v3, /device:TPU:0, one launch (start us, length us, event | category | flops | bytes accessed | tf_op | source)
XLA Modules:
  0.0 21.5 jit_solution(9748972944110804937)
XLA Ops:
  0.0 20.3 %channel.1 = f32[3,32,32,128]{3,2,1,0:T(8,128)S(1)} custom-call(f32[3,32,32,128]{3,2,1,0:T(8,128)} %vel.1), custom_call_target="tpu_custom_call" | custom-call | tf_op jit(solution)/shard_map/channel/pallas_call | solution.py:259
  20.3 1.1 %copy.3 = f32[3,32,32,128]{3,2,1,0:T(8,128)} copy(f32[3,32,32,128]{3,2,1,0:T(8,128)S(1)} %channel.1) | data formatting | bytes 3145728

commit v4 on v3

--- a/solution.py
+++ b/solution.py
@@ -31,9 +31,10 @@
     def peer(hop):
         if n & (n - 1):
             return lax.rem(me + hop, n)
-        other = me
+        other, turn = me, n - hop
+        turn = turn ^ 1 if turn > 1 else turn
         for bit in (1 << i for i in range(n.bit_length() - 1)):
-            if (n - hop) & bit:
+            if turn & bit:
                 other = other + bit - 2 * bit * ((me // bit) % 2)
         return other
 
@@ -65,11 +66,11 @@
     to_before.start()
 
     up = pltpu.make_async_remote_copy(
-        vel.at[:, ny - 1], ext.at[:, 0, pl.ds(TILE, nz)], ys_sem.at[0], yr_sem.at[0],
+        ext.at[:, ny, pl.ds(TILE, nz)], ext.at[:, 0, pl.ds(TILE, nz)], ys_sem.at[0], yr_sem.at[0],
         device_id={"wall": jnp.minimum(me + 1, n - 1)}, device_id_type=MESH,
     )
     down = pltpu.make_async_remote_copy(
-        vel.at[:, 0], ext.at[:, ny + 1, pl.ds(TILE, nz)], ys_sem.at[1], yr_sem.at[1],
+        ext.at[:, 1, pl.ds(TILE, nz)], ext.at[:, ny + 1, pl.ds(TILE, nz)], ys_sem.at[1], yr_sem.at[1],
         device_id={"wall": jnp.maximum(me - 1, 0)}, device_id_type=MESH,
     )
     has_above = me < n - 1

time: 21.6 us -> 22.4 us (1.037)
  Pallas kernels: 20.3 us -> 21.1 us
    pallas_call x1, Pallas kernels: 20.3 us -> 21.1 us  [body(): pl.pallas_call(functools.partial(kernel, n, m), out_shape=jax.ShapeDtypeS...]
where the time goes in v4:
time: 22.4 us; the launch traced here: 22.2 us
  Pallas kernels  21.1 us (94%)
  local copies, waits for them, and re-layouts  1.15 us (5%)
    pallas_call x1, Pallas kernels, body(): pl.pallas_call(functools.partial(kernel, n, m), out_shape=jax.ShapeDtypeS...  21.1 us
    unnamed x1, local copies, waits for them, and re-layouts  1.15 us

profile of v4, /device:TPU:0, one launch (start us, length us, event | category | flops | bytes accessed | tf_op | source)
XLA Modules:
  0.0 22.2 jit_solution(2987808500910286473)
XLA Ops:
  0.0 21.1 %channel.1 = f32[3,32,32,128]{3,2,1,0:T(8,128)S(1)} custom-call(f32[3,32,32,128]{3,2,1,0:T(8,128)} %vel.1), custom_call_target="tpu_custom_call" | custom-call | tf_op jit(solution)/shard_map/channel/pallas_call | solution.py:260
  21.1 1.1 %copy.3 = f32[3,32,32,128]{3,2,1,0:T(8,128)} copy(f32[3,32,32,128]{3,2,1,0:T(8,128)S(1)} %channel.1) | data formatting | bytes 3145728
